TPU v7x, 32 devices: a whole 2x2x4 slice. The times are simulated.
32 devices in a mesh: tower: 2 (over y), dp: 4 (over z), mp: 4 (over x, core).
Axes of the slice: x: 2, y: 2, z: 4, core: 2. Of those that a mesh axis runs over, the one named last changes fastest.
Arguments:
- tokens: bfloat16 [2, 4, 1024, 1024], P('tower', 'dp', 'mp'), may hold values from -6 to 6
- segment_ids: int32 [2, 4, 1024], P(None, 'dp'), may hold values from 0 to 7, never falling along the last dimension, each value on 1 to 512 neighbouring positions
- key_mask: int32 [2, 4, 1024], P(None, 'dp'), may hold values 0 or 1
- positives: int32 [4, 8], replicated, may hold values from 0 to 7, each once within a row
- w_qkv: bfloat16 [1024, 3, 1024], P(None, None, 'mp'), may hold values from -0.1875 to 0.1875
- b_qv: float32 [2, 1024], P(None, 'mp'), may hold values from -3 to 3
- w_out: bfloat16 [1024, 1024], P('mp'), may hold values from -0.75 to 0.75
- b_out: float32 [1024], replicated, may hold values from -2 to 2
- gain_one: float32 [1024], replicated, may hold values from 0.5 to 1.5
- shift_one: float32 [1024], replicated, may hold values from -2 to 2
- w_up: bfloat16 [1024, 4096], P(None, 'mp'), may hold values from -0.1875 to 0.1875
- b_up: float32 [4096], P('mp'), may hold values from -2 to 2
- w_down: bfloat16 [4096, 1024], P('mp'), may hold values from -0.09375 to 0.09375
- b_down: float32 [1024], replicated, may hold values from -2 to 2
- gain_two: float32 [1024], replicated, may hold values from 0.5 to 1.5
- shift_two: float32 [1024], replicated, may hold values from -2 to 2
- w_col: bfloat16 [1024, 1024], P('mp'), may hold values from -0.1875 to 0.1875
- b_col: float32 [1024], replicated, may hold values from -2 to 2
Outputs:
- encoded: bfloat16 [2, 4, 1024, 1024], P('tower', 'dp', 'mp')
- loss: float32 [], replicated
- col_scores: float32 [4, 8, 8], P('dp')
- d_tokens: bfloat16 [2, 4, 1024, 1024], P('tower', 'dp', 'mp')
- grad_qkv: float32 [1024, 3, 1024], P(None, None, 'mp')
- grad_qv_bias: float32 [2, 1024], P(None, 'mp')
- grad_out: float32 [1024, 1024], P('mp')
- grad_out_bias: float32 [1024], replicated
- grad_gain_one: float32 [1024], replicated
- grad_shift_one: float32 [1024], replicated
- grad_up: float32 [1024, 4096], P(None, 'mp')
- grad_up_bias: float32 [4096], P('mp')
- grad_down: float32 [4096, 1024], P('mp')
- grad_down_bias: float32 [1024], replicated
- grad_gain_two: float32 [1024], replicated
- grad_shift_two: float32 [1024], replicated
- grad_col: float32 [1024, 1024], P('mp')
- grad_col_bias: float32 [1024], replicated
Inputs may be any that keep to these rules, and one draw needn't show every extreme that they name: `segment_ids`: in every row segment ids never fall, every id of 0 to 7 is present, and one segment holds exactly 512 tokens. `positives`: each row is a permutation of 0 to 7.
All inputs are finite; a program needn't handle non-finite values. No bound on the sum of `key_mask` on one device may be relied on, other than what follows from the above.
Results may differ from a plain program's by a relative error of at most 0.017.
Values may be sent and summed in bfloat16 or wider, within the bound.
No kernel may reach another device: no remote copies, remote signals or barrier semaphores. Data moves between devices by JAX's collectives and lax.ppermute only.
A program may use at most 128 MiB of HBM per device.

v0:
```python
from functools import partial

import jax
import jax.numpy as jnp
from jax import lax
from jax.sharding import PartitionSpec as P

HEAD_DIM = 64


EPS = 1e-05
NORM_EPS = 1e-06
SCALE_DENSE = 50.0
SCALE_COL = 50.0
SHARP = 20.0
BLOCK_ROWS = 512
HIGH = lax.Precision.HIGHEST


def from_partner(block, axis, stride):
    count = lax.axis_size(axis)
    route = []
    for low in range(count):
        high = low | 1 << stride
        if high != low and high < count:
            route += [(low, high), (high, low)]
    return lax.ppermute(block, axis, route)


def bdot(first_op, second_op):
    return jnp.dot(first_op, second_op, preferred_element_type=jnp.float32)


def fdot(first_op, second_op):
    return jnp.dot(first_op, second_op, precision=HIGH)


def layer_norm(values, gain_vec, shift_vec):
    row_mean = jnp.mean(values, axis=-1, keepdims=True)
    centred = values - row_mean
    spread = jnp.mean(centred * centred, axis=-1, keepdims=True)
    return centred * lax.rsqrt(spread + EPS) * gain_vec + shift_vec


def unit_rows(values):
    return values * lax.rsqrt(jnp.sum(values * values, axis=-1, keepdims=True) + NORM_EPS)


def row_tables(seg_row, mask_row, labels):
    length = seg_row.shape[0]
    member = seg_row[None, :] == labels[:, None]
    starts = jnp.sum((seg_row[None, :] < labels[:, None]).astype(jnp.int32), axis=1)
    places = jnp.arange(length, dtype=jnp.int32)
    cls_pick = places[None, :] == starts[:, None]
    is_valid = jnp.logical_or(mask_row > 0, jnp.any(cls_pick, axis=0))
    return (member, cls_pick, is_valid)


def cross_entropy(logits, targets):
    columns = jnp.arange(logits.shape[1], dtype=jnp.int32)
    onehot = (targets[:, None] == columns[None, :]).astype(jnp.float32)
    row_top = jnp.max(logits, axis=1, keepdims=True)
    exp_terms = jnp.exp(logits - row_top)
    row_total = jnp.sum(exp_terms, axis=1, keepdims=True)
    loss_sum = jnp.sum(row_top[:, 0] + jnp.log(row_total[:, 0]) - jnp.sum(logits * onehot, axis=1))
    return (loss_sum, exp_terms / row_total - onehot)


def attend_forward(query_rows, key_rows, value_rows, seg_row, is_valid):
    length = query_rows.shape[0]
    head_count = query_rows.shape[1] // HEAD_DIM
    block_rows = min(BLOCK_ROWS, length)
    blocks = length // block_rows
    key_heads = key_rows.reshape(length, head_count, HEAD_DIM)
    value_heads = value_rows.reshape(length, head_count, HEAD_DIM)

    def one_block(inputs):
        query_block, seg_block = inputs
        raw_scores = (
            jnp.einsum("qhd,khd->hqk", query_block, key_heads, preferred_element_type=jnp.float32)
            * 0.125
        )
        allowed = jnp.logical_and(seg_block[:, None] == seg_row[None, :], is_valid[None, :])
        masked = jnp.where(allowed[None], raw_scores, -1e30)
        row_top = jnp.max(masked, axis=-1, keepdims=True)
        exp_terms = jnp.exp(masked - row_top)
        row_total = jnp.sum(exp_terms, axis=-1, keepdims=True)
        attn_probs = (exp_terms / row_total).astype(jnp.bfloat16)
        mixed_out = jnp.einsum(
            "hqk,khd->qhd", attn_probs, value_heads, preferred_element_type=jnp.float32
        )
        return (mixed_out.astype(jnp.bfloat16), (row_top + jnp.log(row_total))[..., 0])

    mixed_all, log_total = lax.map(
        one_block,
        (
            query_rows.reshape(blocks, block_rows, head_count, HEAD_DIM),
            seg_row.reshape(blocks, block_rows),
        ),
    )
    return (mixed_all.reshape(length, head_count * HEAD_DIM), log_total)


def attend_backward(query_rows, key_rows, value_rows, grad_mixed, seg_row, is_valid, log_total):
    length = query_rows.shape[0]
    head_count = query_rows.shape[1] // HEAD_DIM
    block_rows = min(BLOCK_ROWS, length)
    blocks = length // block_rows
    key_heads = key_rows.reshape(length, head_count, HEAD_DIM)
    value_heads = value_rows.reshape(length, head_count, HEAD_DIM)

    def one_block(carry, inputs):
        key_acc, value_acc = carry
        query_block, seg_block, grad_block, total_block = inputs
        raw_scores = (
            jnp.einsum("qhd,khd->hqk", query_block, key_heads, preferred_element_type=jnp.float32)
            * 0.125
        )
        allowed = jnp.logical_and(seg_block[:, None] == seg_row[None, :], is_valid[None, :])
        masked = jnp.where(allowed[None], raw_scores, -1e30)
        attn_probs = jnp.exp(masked - total_block[..., None])
        grad_probs = jnp.einsum(
            "qhd,khd->hqk", grad_block, value_heads, preferred_element_type=jnp.float32
        )
        row_dot = jnp.sum(attn_probs * grad_probs, axis=-1, keepdims=True)
        grad_scores = (attn_probs * (grad_probs - row_dot)).astype(jnp.bfloat16)
        grad_query = (
            jnp.einsum("hqk,khd->qhd", grad_scores, key_heads, preferred_element_type=jnp.float32)
            * 0.125
        )
        key_acc = (
            key_acc
            + jnp.einsum(
                "hqk,qhd->khd", grad_scores, query_block, preferred_element_type=jnp.float32
            )
            * 0.125
        )
        value_acc = value_acc + jnp.einsum(
            "hqk,qhd->khd",
            attn_probs.astype(jnp.bfloat16),
            grad_block,
            preferred_element_type=jnp.float32,
        )
        return ((key_acc, value_acc), grad_query.astype(jnp.bfloat16))

    zero_acc = jnp.zeros((length, head_count, HEAD_DIM), jnp.float32)
    shaped = (blocks, block_rows, head_count, HEAD_DIM)
    (key_acc, value_acc), grad_query = lax.scan(
        one_block,
        (zero_acc, zero_acc),
        (
            query_rows.reshape(shaped),
            seg_row.reshape(blocks, block_rows),
            grad_mixed.reshape(shaped),
            log_total,
        ),
    )
    flat_shape = (length, head_count * HEAD_DIM)
    return (
        grad_query.reshape(flat_shape),
        key_acc.reshape(flat_shape).astype(jnp.bfloat16),
        value_acc.reshape(flat_shape).astype(jnp.bfloat16),
    )


def per_device(
    tokens,
    segment_ids,
    key_mask,
    positives,
    w_qkv,
    b_qv,
    w_out,
    b_out,
    gain_one,
    shift_one,
    w_up,
    b_up,
    w_down,
    b_down,
    gain_two,
    shift_two,
    w_col,
    b_col,
):
    own_rows = tokens[0, 0]
    own_count = own_rows.shape[0]
    model_dim = own_rows.shape[1]
    mp_size = lax.axis_size("mp")
    mp_index = lax.axis_index("mp")
    tower_size = lax.axis_size("tower")
    tower_index = lax.axis_index("tower")
    dp_index = lax.axis_index("dp")
    seg_count = positives.shape[1]
    labels = jnp.arange(seg_count, dtype=jnp.int32)
    seg_pair = segment_ids[:, 0]
    mask_pair = key_mask[:, 0]
    seg_row = lax.dynamic_index_in_dim(seg_pair, tower_index, 0, keepdims=False)
    mask_row = lax.dynamic_index_in_dim(mask_pair, tower_index, 0, keepdims=False)
    length = seg_row.shape[0]
    member, cls_pick, is_valid = row_tables(seg_row, mask_row, labels)
    full_x, col_weight = (
        lax.all_gather(own_rows, "mp", axis=0, tiled=True),
        lax.all_gather(w_col, "mp", axis=0, tiled=True),
    )
    projected = jnp.einsum("ld,dch->lch", full_x, w_qkv, preferred_element_type=jnp.float32)
    query_rows = (projected[:, 0] + b_qv[0]).astype(jnp.bfloat16)
    key_rows = projected[:, 1].astype(jnp.bfloat16)
    value_rows = (projected[:, 2] + b_qv[1]).astype(jnp.bfloat16)
    context, log_total = attend_forward(query_rows, key_rows, value_rows, seg_row, is_valid)
    attn_sum = lax.psum(bdot(context, w_out), "mp")
    pre_all = full_x.astype(jnp.float32) + attn_sum + b_out
    hidden_full = layer_norm(pre_all, gain_one, shift_one).astype(jnp.bfloat16)
    pre_own = lax.dynamic_slice_in_dim(pre_all, mp_index * own_count, own_count, 0)
    hidden, norm_one_back = jax.vjp(layer_norm, pre_own, gain_one, shift_one)
    inner_act = bdot(hidden_full, w_up) + b_up
    active = jax.nn.gelu(inner_act, approximate=False).astype(jnp.bfloat16)
    ffn_out = lax.psum_scatter(bdot(active, w_down), "mp", scatter_dimension=0, tiled=True)
    final_rows, norm_two_back = jax.vjp(layer_norm, hidden + ffn_out + b_down, gain_two, shift_two)
    encoded = final_rows.astype(jnp.bfloat16)
    col_pre = bdot(encoded, col_weight) + b_col
    col_unit, col_back = jax.vjp(unit_rows, col_pre)
    col_vec = col_unit.astype(jnp.bfloat16)
    own_pick = lax.dynamic_slice_in_dim(
        cls_pick.astype(jnp.float32), mp_index * own_count, own_count, 1
    )
    cls_raw = fdot(own_pick, final_rows)
    cls_unit, cls_back = jax.vjp(unit_rows, cls_raw)
    pair_vec, pair_cls = (
        lax.all_gather(col_vec, ("tower", "mp"), axis=0, tiled=True),
        lax.all_gather(cls_unit.astype(jnp.bfloat16), ("tower", "mp"), axis=0, tiled=True),
    )
    cls_pair = jnp.sum(
        pair_cls.astype(jnp.float32).reshape(tower_size, mp_size, seg_count, model_dim), axis=1
    ).astype(jnp.bfloat16)
    all_cls = lax.all_gather(
        cls_pair.reshape(tower_size * seg_count, model_dim), "dp", axis=0, tiled=True
    )
    group_count = all_cls.shape[0] // (tower_size * seg_count)
    cls_table = all_cls.reshape(group_count, tower_size, seg_count, model_dim)
    queries = cls_table[:, 0].reshape(group_count * seg_count, model_dim)
    passages = cls_table[:, 1].reshape(group_count * seg_count, model_dim)
    dense_logits = bdot(queries, passages.T) * SCALE_DENSE
    targets = (jnp.arange(group_count, dtype=jnp.int32)[:, None] * seg_count + positives).reshape(
        group_count * seg_count
    )
    dense_loss, dense_grad = cross_entropy(dense_logits, targets)
    dense_grad_b = (dense_grad / seg_count).astype(jnp.bfloat16)
    own_first = dp_index * seg_count
    grad_q_own = (
        bdot(lax.dynamic_slice_in_dim(dense_grad_b, own_first, seg_count, 0), passages)
        * SCALE_DENSE
    )
    grad_p_own = (
        bdot(lax.dynamic_slice_in_dim(dense_grad_b, own_first, seg_count, 1).T, queries)
        * SCALE_DENSE
    )
    grad_cls_unit = jnp.where(tower_index == 0, grad_q_own, grad_p_own)
    grad_cls_raw = cls_back(grad_cls_unit)[0]
    grad_final = fdot(own_pick.T, grad_cls_raw)
    member_q, pick_q, valid_q = row_tables(seg_pair[0], mask_pair[0], labels)
    member_p, pick_p, valid_p = row_tables(seg_pair[1], mask_pair[1], labels)
    weight_q = jnp.logical_and(member_q, valid_q[None, :]).astype(jnp.float32)
    weight_p = jnp.logical_and(member_p, valid_p[None, :]).astype(jnp.float32)
    seg_sizes = jnp.sum(weight_q, axis=1, keepdims=True)
    slot_count = tower_size * mp_size
    span_rows = length // slot_count
    slot_index = mp_index * tower_size + tower_index
    query_vecs = lax.dynamic_slice_in_dim(pair_vec, slot_index * span_rows, span_rows, 0)
    passage_vecs = pair_vec[length:]
    similar = bdot(query_vecs, passage_vecs.T)
    exp_terms = jnp.exp(SHARP * similar)
    sum_terms = fdot(exp_terms, weight_p.T)
    nearest = jnp.log(sum_terms) / SHARP
    weight_block = (
        lax.dynamic_slice_in_dim(weight_q, slot_index * span_rows, span_rows, 1) / seg_sizes
    )
    partial_score = fdot(weight_block, nearest)
    pair_total = lax.psum(partial_score, ("tower", "mp"))
    positive_row = lax.dynamic_index_in_dim(positives, dp_index, 0, keepdims=False)
    col_loss, col_grad = cross_entropy(pair_total * SCALE_COL, positive_row)
    grad_pair = col_grad / seg_count * SCALE_COL
    grad_nearest = fdot(weight_block.T, grad_pair)
    grad_sums = grad_nearest / (SHARP * sum_terms)
    grad_similar = (fdot(grad_sums, weight_p) * exp_terms * SHARP).astype(jnp.bfloat16)
    grad_query_vecs = bdot(grad_similar, passage_vecs)
    grad_passage_vecs = bdot(grad_similar.T, query_vecs)
    passage_part = lax.psum_scatter(grad_passage_vecs, "mp", scatter_dimension=0, tiled=True)
    partner_query, partner_passage = from_partner((grad_query_vecs, passage_part), "tower", 0)
    query_whole = jnp.concatenate([grad_query_vecs, partner_query], axis=0)
    vector_grad = jnp.where(tower_index == 0, query_whole, passage_part + partner_passage)
    grad_col_pre = col_back(vector_grad)[0].astype(jnp.bfloat16)
    grad_final = grad_final + bdot(grad_col_pre, col_weight.T)
    grad_col_full = bdot(encoded.T, grad_col_pre)
    grad_col_bias = jnp.sum(grad_col_pre.astype(jnp.float32), axis=0)
    grad_resid_two, grad_gain_two, grad_shift_two = norm_two_back(grad_final)
    grad_down_bias = jnp.sum(grad_resid_two, axis=0)
    grad_ffn_full = lax.all_gather(grad_resid_two.astype(jnp.bfloat16), "mp", axis=0, tiled=True)
    grad_active = bdot(grad_ffn_full, w_down.T)
    grad_down = bdot(active.T, grad_ffn_full)
    gelu_value, gelu_back = jax.vjp(partial(jax.nn.gelu, approximate=False), inner_act)
    grad_inner = gelu_back(grad_active)[0].astype(jnp.bfloat16)
    grad_up = bdot(hidden_full.T, grad_inner)
    grad_up_bias = jnp.sum(grad_inner.astype(jnp.float32), axis=0)
    hidden_terms = bdot(grad_inner, w_up.T)
    hidden_share, grad_col_share = (
        lax.psum_scatter(hidden_terms, "mp", scatter_dimension=0, tiled=True),
        lax.psum_scatter(grad_col_full, "mp", scatter_dimension=0, tiled=True),
    )
    grad_hidden = grad_resid_two + hidden_share
    grad_resid_one, grad_gain_one, grad_shift_one = norm_one_back(grad_hidden)
    grad_out_bias = jnp.sum(grad_resid_one, axis=0)
    grad_attn_full = lax.all_gather(grad_resid_one.astype(jnp.bfloat16), "mp", axis=0, tiled=True)
    grad_out = bdot(context.T, grad_attn_full)
    grad_context = bdot(grad_attn_full, w_out.T).astype(jnp.bfloat16)
    grad_query, grad_key, grad_value = attend_backward(
        query_rows, key_rows, value_rows, grad_context, seg_row, is_valid, log_total
    )
    grad_proj = jnp.stack([grad_query, grad_key, grad_value], axis=1)
    grad_qkv = jnp.einsum("ld,lch->dch", full_x, grad_proj, preferred_element_type=jnp.float32)
    grad_qv_bias = jnp.stack(
        [
            jnp.sum(grad_query.astype(jnp.float32), axis=0),
            jnp.sum(grad_value.astype(jnp.float32), axis=0),
        ]
    )
    grad_input = grad_resid_one + lax.psum_scatter(
        jnp.einsum("lch,dch->ld", grad_proj, w_qkv, preferred_element_type=jnp.float32),
        "mp",
        scatter_dimension=0,
        tiled=True,
    )
    d_tokens = grad_input.astype(jnp.bfloat16).reshape(1, 1, own_count, model_dim)
    sharded = lax.psum(
        (grad_qkv, grad_qv_bias, grad_out, grad_up, grad_up_bias, grad_down, grad_col_share),
        ("tower", "dp"),
    )
    loss_share = col_loss / (seg_count * tower_size * mp_size)
    shared = lax.psum(
        (
            grad_col_bias,
            grad_out_bias,
            grad_gain_one,
            grad_shift_one,
            grad_down_bias,
            grad_gain_two,
            grad_shift_two,
            loss_share,
        ),
        ("tower", "dp", "mp"),
    )
    loss_sum = dense_loss / seg_count + shared[7]
    col_scores = pair_total.reshape(1, seg_count, seg_count)
    return (
        encoded.reshape(1, 1, own_count, model_dim),
        loss_sum,
        col_scores,
        d_tokens,
        sharded[0],
        sharded[1],
        sharded[2],
        shared[1],
        shared[2],
        shared[3],
        sharded[3],
        sharded[4],
        sharded[5],
        shared[4],
        shared[5],
        shared[6],
        sharded[6],
        shared[0],
    )


def solution(mesh):
    return jax.shard_map(
        per_device,
        mesh=mesh,
        in_specs=(
            P("tower", "dp", "mp", None),
            P(None, "dp", None),
            P(None, "dp", None),
            P(),
            P(None, None, "mp"),
            P(None, "mp"),
            P("mp", None),
            P(),
            P(),
            P(),
            P(None, "mp"),
            P("mp"),
            P("mp", None),
            P(),
            P(),
            P(),
            P("mp", None),
            P(),
        ),
        out_specs=(
            P("tower", "dp", "mp", None),
            P(),
            P("dp", None, None),
            P("tower", "dp", "mp", None),
            P(None, None, "mp"),
            P(None, "mp"),
            P("mp", None),
            P(),
            P(),
            P(),
            P(None, "mp"),
            P("mp"),
            P("mp", None),
            P(),
            P(),
            P(),
            P("mp", None),
            P(),
        ),
        check_vma=False,
    )
```

profile of v0, /device:TPU:0, one launch (start us, length us, event | category | flops | bytes accessed | tf_op | source)
XLA Modules:
  0.0 1062.7 jit_solution(12393578077360360568)
XLA Ops:
  11.9 23.0 %all-gather.15.cloned.1.call-done = bf16[1,1,1024,1024]{3,2,1,0:T(8,128)(2,1)} async-done(((bf16[1,1,256,1024]{3,2,1,0:T(8,128)(2,1)}), bf16[1,1,1024,1024]{3,2,1,0:T(8,128)(2,1)}) %all-gather.15.cloned.1.call-update) | async-done | bytes 2097168 | tf_op jit(solution)/shard_map/all_gather | solution.py:203
  34.9 3.9 fusion.51
  47.9 16.6 %while.27 = (s32[]{:T(128)}, bf16[2,512,4,64]{1,3,2,0:T(8,128)(2,1)}, f32[2,4,512]{2,1,0:T(4,128)S(1)}, s32[2,512]{1,0:T(2,128)S(1)}, s32[1024]{0:T(1024)S(1)}, ...) while((s32[]{:T(128)}, ...), condition=%wide.region_5.6_spmd, body=%wide.region_2.5_spmd.sunk | while | flops 563214336 | bytes 35204304 | solution.py:94
  67.0 3.8 fusion.143
  71.3 85.1 %all-reduce.6.cloned.1.call-done = f32[1024,1024]{1,0:T(8,128)} async-done(((f32[1024,1024]{1,0:T(8,128)}), f32[1024,1024]{1,0:T(8,128)}) %all-reduce.6.cloned.1.call-update) | async-done | bytes 4194320 | tf_op jit(solution)/shard_map/psum | solution.py:211
  160.8 13.1 %multiply_convert_fusion.1 = (bf16[1024,1024]{1,0:T(8,128)(2,1)S(1)}, f32[1024,1024]{1,0:T(8,128)}, f32[1024,1024]{1,0:T(8,128)}) fusion(f32[1024]{0:T(1024)S(1)} %copy-done.76, bf16[1024,1024]{1,0:T(8,128)(2,1)S(1)} %copy-done, f32[1024,1024]{1,0:T(8,128)S(1)} %get-tuple-element.354, f32[1024]{0:T(1024)S(1)} %copy-done.59, f32[1024]{0:T(1024)S(1)} %copy-done.43, ...), kind=kOutput, calls=%fused_computation.56 | convolution fusion | flops 2221932544 | bytes 16797696 | tf_op jit(solution)/shard_map/dot_general | solution.py:31
  175.2 4.3 fusion.144
  183.1 41.3 %reduce-scatter.6.cloned.1.call-done = f32[256,1024]{1,0:T(8,128)} async-done(((f32[1024,1024]{1,0:T(8,128)}), f32[256,1024]{1,0:T(8,128)}) %reduce-scatter.6.cloned.1.call-update) | async-done | bytes 1048592 | tf_op jit(solution)/shard_map/reduce_scatter | solution.py:218
  227.6 20.8 %all-gather.7.cloned.1.call-done = bf16[1024,1024]{1,0:T(8,128)(2,1)} async-done(((bf16[256,1024]{1,0:T(8,128)(2,1)}), bf16[1024,1024]{1,0:T(8,128)(2,1)}) %all-gather.7.cloned.1.call-update) | async-done | bytes 2097168 | tf_op jit(solution)/shard_map/all_gather | solution.py:204
  253.8 36.2 %all-gather.9.cloned.1.call-done = bf16[2048,1024]{1,0:T(8,128)(2,1)} async-done(((bf16[256,1024]{1,0:T(8,128)(2,1)}), bf16[2048,1024]{1,0:T(8,128)(2,1)}) %all-gather.9.cloned.1.call-update) | async-done | bytes 4194320 | tf_op jit(solution)/shard_map/all_gather | solution.py:230
  293.9 13.1 %psum.120 = f32[8,8]{1,0:T(8,128)S(1)} all-reduce(f32[8,8]{1,0:T(8,128)S(1)} %fusion.107), channel_id=1, replica_groups=mesh['tower'=2,'dp'=4,'mp'=4] {'tower','mp'}, use_global_device_ids=true, to_apply=%region_26.27 | all-reduce | flops 64 | bytes 512 | tf_op jit(solution)/shard_map/psum | solution.py:279
  309.6 3.7 fusion.79
  315.6 10.1 all_gather.22
  326.7 13.7 %all_gather.23 = bf16[64,1024]{1,0:T(8,128)(2,1)S(1)} all-gather(bf16[16,1024]{1,0:T(8,128)(2,1)S(1)} %bitcast.186), channel_id=1, replica_groups=mesh['tower'=2,'dp'=4,'mp'=4] {'dp'}, dimensions={0}, use_global_device_ids=true | all-gather | bytes 163840 | tf_op jit(solution)/shard_map/all_gather | solution.py:236
  341.7 16.2 %reduce-scatter.8.cloned.1.call-done = f32[256,1024]{1,0:T(8,128)} async-done(((f32[1024,1024]{1,0:T(8,128)}), f32[256,1024]{1,0:T(8,128)}) %reduce-scatter.8.cloned.1.call-update) | async-done | bytes 1048592 | tf_op jit(solution)/shard_map/reduce_scatter | solution.py:288
  365.1 29.2 %collective-permute-done = f32[128,1024]{1,0:T(8,128)S(1)} collective-permute-done((f32[128,1024]{1,0:T(8,128)S(1)}, f32[128,1024]{1,0:T(8,128)S(1)}, u32[]{:S(2)}, u32[]{:S(2)}) %collective-permute-start) | collective-permute-done | bytes 524320 | tf_op jit(solution)/shard_map/ppermute | solution.py:27
  402.6 22.7 %all-gather.11.cloned.1.call-done = bf16[1024,1024]{1,0:T(8,128)(2,1)} async-done(((bf16[256,1024]{1,0:T(8,128)(2,1)}), bf16[1024,1024]{1,0:T(8,128)(2,1)}) %all-gather.11.cloned.1.call-update) | async-done | bytes 2097168 | tf_op jit(solution)/shard_map/all_gather | solution.py:298
  425.3 8.3 convert_reduce_fusion
  435.0 4.4 fusion.146
  439.5 44.6 %reduce-scatter.10.cloned.1.call-done = f32[256,1024]{1,0:T(8,128)} async-done(((f32[1024,1024]{1,0:T(8,128)}), f32[256,1024]{1,0:T(8,128)}) %reduce-scatter.10.cloned.1.call-update) | async-done | bytes 1048592 | tf_op jit(solution)/shard_map/reduce_scatter | solution.py:307
  489.0 3.9 fusion.149
  493.0 18.7 %all-gather.13.cloned.1.call-done = bf16[1024,1024]{1,0:T(8,128)(2,1)} async-done(((bf16[256,1024]{1,0:T(8,128)(2,1)}), bf16[1024,1024]{1,0:T(8,128)(2,1)}) %all-gather.13.cloned.1.call-update) | async-done | bytes 2097168 | tf_op jit(solution)/shard_map/all_gather | solution.py:313
  520.9 25.4 %while.28 = (s32[]{:T(128)}, f32[1024,4,64]{0,2,1:T(8,128)S(1)}, f32[1024,4,64]{0,2,1:T(8,128)}, bf16[2,512,4,64]{1,3,2,0:T(8,128)(2,1)}, bf16[2,512,4,64]{1,3,2...) while((s32[]{:T(128)}, f32[1024,4,64]{0,2,1:T(8,128)S(1)}, ...), condition=%wide.region_42.43_spmd.clone, body=%wide.region_40.42_spmd.clone.sunk | while | flops 1376253952 | bytes 86838592 | solution.py:148
  550.4 5.4 convolution_bitcast_fusion
  557.4 6.2 fusion.148
  563.6 4.8 fusion.132
  578.3 22.5 %all-reduce.1 = (f32[2,256]{1,0:T(2,128)}, f32[1024]{0:T(1024)}) all-reduce(f32[2,256]{1,0:T(2,128)S(1)} %pad_maximum_fusion.3, f32[1024]{0:T(1024)S(1)} %get-tuple-element.336), channel_id=1, replica_groups=mesh['tower'=2,'dp'=4,'mp'=4] {'tower','dp'}, use_global_device_ids=true, to_apply=%region_47.48 | all-reduce | flops 1536 | bytes 12288 | tf_op jit(solution)/shard_map/psum | solution.py:334
  600.7 5.7 reduce-scatter.12.cloned.1.call-done
  608.6 45.1 %all-reduce = (f32[]{:T(128)}, f32[1024]{0:T(1024)}, f32[1024]{0:T(1024)}, f32[1024]{0:T(1024)}, f32[1024]{0:T(1024)}, /*index=5*/f32[1024]{0:T(1024)}, f32[1024]{0:T(1024)}, f32[1024]{0:T(1024)}) all-reduce(f32[]{:T(128)S(6)} %div.116, ...), channel_id=1, replica_groups=mesh['tower'=2,'dp'=4,'mp'=4] {'tower','dp','mp'}, use_global_device_ids=true, to_apply=%region_31.32 | all-reduce | flops 7169 | bytes 57352 | tf_op jit(solution)/shard_map/psum | solution.py:339
  654.4 387.3 %all-reduce.8.cloned.1.call-done = (f32[1024,3,256]{0,2,1:T(8,128)}, f32[256,1024]{1,0:T(8,128)}, f32[1024,1024]{1,0:T(8,128)}, f32[1024,1024]{1,0:T(8,128)}, f32[256,1024]{1,0:T(8,128)}) async-done(((f32[1024,3,256]{0,2,1:T(8,128)}, f32[256,1024]{1,0:T(8,128)}, f32[1024,1024]{1,0:T(8,128)}, f32[1024,1024]{1,0:T(8,128)}, f32[256,1024]{1,0:T(8,128)}), (f32[1024,3,256]{0,2,1:T(8,128)}, f32[256,1024]{1,0:T(8,128)}, ...) | async-done | bytes 13631504 | tf_op jit(solution)/shard_map/psum | solution.py:334
  1041.7 3.6 copy.65
  1046.3 4.9 copy.108
  (339 shorter events, 137.9 us)
Async XLA Ops:
  7.2 153.4 %copy-start = (bf16[1024,1024]{1,0:T(8,128)(2,1)S(1)}, bf16[1024,1024]{1,0:T(8,128)(2,1)}, u32[]{:S(2)}) copy-start(bf16[1024,1024]{1,0:T(8,128)(2,1)} %param.32) | copy-start | bytes 6291460
  7.2 27.7 %all-gather.15.cloned.1.call-start = ((), (), s32[]{:S(2)}) async-start(), calls=%async_computation.15 | async-start | bytes 2621440 | tf_op jit(solution)/shard_map/all_gather | solution.py:203
  7.9 148.5 %all-reduce.6.cloned.1.call-start = ((), (), s32[]{:S(2)}) async-start(), calls=%async_computation.5 | async-start | bytes 8388608 | tf_op jit(solution)/shard_map/psum | solution.py:211
  70.8 85.7 %copy-start.57 = (f32[1024]{0:T(1024)S(1)}, f32[1024]{0:T(1024)}, u32[]{:S(2)}) copy-start(f32[1024]{0:T(1024)} %param.29) | copy-start | bytes 12292
  70.8 153.6 %reduce-scatter.6.cloned.1.call-start = ((), (), s32[]{:S(2)}) async-start(), calls=%async_computation.6 | async-start | bytes 5242880 | tf_op jit(solution)/shard_map/reduce_scatter | solution.py:218
  179.5 44.8 %copy-start.58 = (f32[1024]{0:T(1024)S(1)}, f32[1024]{0:T(1024)}, u32[]{:S(2)}) copy-start(f32[1024]{0:T(1024)} %param.35) | copy-start | bytes 12292
  179.6 68.9 %copy-start.41 = (f32[1024]{0:T(1024)S(1)}, f32[1024]{0:T(1024)}, u32[]{:S(2)}) copy-start(f32[1024]{0:T(1024)} %param.36) | copy-start | bytes 12292
  179.6 68.8 %copy-start.44 = (f32[1024]{0:T(1024)S(1)}, f32[1024]{0:T(1024)}, u32[]{:S(2)}) copy-start(f32[1024]{0:T(1024)} %param.37) | copy-start | bytes 12292
  179.6 68.8 %copy-start.75 = (f32[1024]{0:T(1024)S(1)}, f32[1024]{0:T(1024)}, u32[]{:S(2)}) copy-start(f32[1024]{0:T(1024)} %param.39) | copy-start | bytes 12292
  179.6 68.8 %all-gather.7.cloned.1.call-start = ((), (), s32[]{:S(2)}) async-start(), calls=%async_computation.7 | async-start | bytes 2621440 | tf_op jit(solution)/shard_map/all_gather | solution.py:204
  180.2 109.8 %all-gather.9.cloned.1.call-start = ((), (), s32[]{:S(2)}) async-start(), calls=%async_computation.8 | async-start | bytes 4718592 | tf_op jit(solution)/shard_map/all_gather | solution.py:230
  251.2 62.0 %copy-start.61 = (f32[256]{0:T(256)}, f32[256]{0:T(256)S(1)}, u32[]{:S(2)}) copy-start(f32[256]{0:T(256)S(1)} %get-tuple-element.376) | copy-start | bytes 3076
  253.1 104.8 %reduce-scatter.8.cloned.1.call-start = ((), (), s32[]{:S(2)}) async-start(), calls=%async_computation.9 | async-start | bytes 5242880 | tf_op jit(solution)/shard_map/reduce_scatter | solution.py:288
  313.3 112.0 %all-gather.11.cloned.1.call-start = ((), (), s32[]{:S(2)}) async-start(), calls=%async_computation.10 | async-start | bytes 2621440 | tf_op jit(solution)/shard_map/all_gather | solution.py:298
  341.2 55.1 %copy-start.53 = (f32[32]{0:T(128)}, f32[32]{0:T(128)S(1)}, u32[]{:S(2)}) copy-start(f32[32]{0:T(128)S(1)} %get-tuple-element.374) | copy-start | bytes 388
  341.7 54.6 %copy-start.55 = (f32[32]{0:T(128)}, f32[32]{0:T(128)S(1)}, u32[]{:S(2)}) copy-start(f32[32]{0:T(128)S(1)} %get-tuple-element.270) | copy-start | bytes 388
  358.0 36.4 %collective-permute-start.1 = (f32[256,1024]{1,0:T(8,128)}, f32[256,1024]{1,0:T(8,128)S(1)}, u32[]{:S(2)}, u32[]{:S(2)}) collective-permute-start(f32[256,1024]{1,0:T(8,128)} %reduce-scatter.8.cloned.1.call-done), channel_id=1, source_target_pairs={{0,16},{16,0},{1,17},{17,1},{2,18},{18,2},{3,19},{19,3},{4,20},{20... | collective-permute-start | bytes 3145736 | tf_op jit(solution)/shard_map/ppermute | solution.py:27
  359.5 36.9 %copy-start.62 = (f32[256]{0:T(256)S(1)}, f32[256]{0:T(256)}, u32[]{:S(2)}) copy-start(f32[256]{0:T(256)} %copy-done.61) | copy-start | bytes 3076
  359.5 36.9 %copy-start.15 = (f32[256,1024]{1,0:T(8,128)S(1)}, f32[256,1024]{1,0:T(8,128)}, u32[]{:S(2)}) copy-start(f32[256,1024]{1,0:T(8,128)} %copy-done.14) | copy-start | bytes 3145732
  361.6 35.6 %copy-start.24 = (bf16[1024,1024]{1,0:T(8,128)(2,1)S(1)}, bf16[1024,1024]{1,0:T(8,128)(2,1)}, u32[]{:S(2)}) copy-start(bf16[1024,1024]{1,0:T(8,128)(2,1)} %all-gather.7.cloned.1.call-done) | copy-start | bytes 6291460
  361.6 32.7 %collective-permute-start = (f32[128,1024]{1,0:T(8,128)S(1)}, f32[128,1024]{1,0:T(8,128)S(1)}, u32[]{:S(2)}, u32[]{:S(2)}) collective-permute-start(f32[128,1024]{1,0:T(8,128)S(1)} %fusion.56), channel_id=1, source_target_pairs={{0,16},{16,0},{1,17},{17,1},{2,18},{18,2},{3,19},{19,3},{4,20},{20... | collective-permute-start | bytes 1572872 | tf_op jit(solution)/shard_map/ppermute | solution.py:27
  402.6 81.5 %reduce-scatter.10.cloned.1.call-start = ((), (), s32[]{:S(2)}) async-start(), calls=%async_computation.11 | async-start | bytes 5242880 | tf_op jit(solution)/shard_map/reduce_scatter | solution.py:307
  439.4 44.7 %copy-start.11 = (f32[256,1024]{1,0:T(8,128)S(1)}, f32[256,1024]{1,0:T(8,128)}, u32[]{:S(2)}) copy-start(f32[256,1024]{1,0:T(8,128)} %copy-done.10) | copy-start | bytes 3145732
  439.4 49.6 %copy-start.4 = (f32[256,1024]{1,0:T(8,128)S(1)}, f32[256,1024]{1,0:T(8,128)}, u32[]{:S(2)}) copy-start(f32[256,1024]{1,0:T(8,128)} %copy-done.2) | copy-start | bytes 3145732
  439.4 72.3 %all-gather.13.cloned.1.call-start = ((), (), s32[]{:S(2)}) async-start(), calls=%async_computation.12 | async-start | bytes 2621440 | tf_op jit(solution)/shard_map/all_gather | solution.py:313
  489.0 84.7 %reduce-scatter.14.cloned.1.call-start = ((), (), s32[]{:S(2)}) async-start(), calls=%async_computation.14 | async-start | bytes 5242880 | tf_op jit(solution)/shard_map/reduce_scatter | solution.py:308
  493.0 113.4 %reduce-scatter.12.cloned.1.call-start = ((), (), s32[]{:S(2)}) async-start(), calls=%async_computation.13 | async-start | bytes 5242880 | tf_op jit(solution)/shard_map/reduce_scatter | solution.py:327
  555.9 485.9 %all-reduce.8.cloned.1.call-start = ((), (), s32[]{:S(2)}) async-start(), calls=%async_computation.16 | async-start | bytes 27262976 | tf_op jit(solution)/shard_map/psum | solution.py:334
  573.8 34.9 %copy-start.45 = (f32[1024]{0:T(1024)S(1)}, f32[1024]{0:T(1024)}, u32[]{:S(2)}) copy-start(f32[1024]{0:T(1024)} %get-tuple-element.340) | copy-start | bytes 12292
  573.8 34.8 %copy-start.46 = (f32[1024]{0:T(1024)S(1)}, f32[1024]{0:T(1024)}, u32[]{:S(2)}) copy-start(f32[1024]{0:T(1024)} %get-tuple-element.266) | copy-start | bytes 12292
  573.8 34.8 %copy-start.47 = (f32[1024]{0:T(1024)S(1)}, f32[1024]{0:T(1024)}, u32[]{:S(2)}) copy-start(f32[1024]{0:T(1024)} %get-tuple-element.268) | copy-start | bytes 12292
  573.8 34.8 %copy-start.48 = (f32[1024]{0:T(1024)S(1)}, f32[1024]{0:T(1024)}, u32[]{:S(2)}) copy-start(f32[1024]{0:T(1024)} %get-tuple-element.365) | copy-start | bytes 12292
  (71 other events, 389.5 us)
Sparse Core Ops, SparseCore 0:
  9.6 25.2 all-gather.14
  70.9 85.4 all-reduce.5
  179.7 44.6 reduce-scatter.5
  225.8 22.5 all-gather.6
  253.2 36.7 all-gather.8
  313.4 44.5 reduce-scatter.7
  402.7 22.5 all-gather.10
  439.5 44.4 reduce-scatter.9
  489.1 22.5 all-gather.12
  514.1 44.4 reduce-scatter.13
  561.9 44.4 reduce-scatter.11
  612.6 429.1 all-reduce.7
where the time goes:
time: 1070 us; the launch traced here: 1060 us
  waiting for transfers between devices  732 us (68%)
  matrix products  115 us (11%)
  blocking collectives  105 us (10%)
  local copies, waits for them, and re-layouts  45 us (4%)
  other arithmetic  44 us (4%)
  between operations  18.7 us (2%)
    psum x1, waiting for transfers between devices, per_device(): lax.psum((grad_qkv, grad_qv_bias, grad_out, grad_up, grad_up_bias, grad_d...  387 us
    psum x1, waiting for transfers between devices, per_device(): attn_sum = lax.psum(bdot(context, w_out), 'mp')  85.1 us
    dot_general x18, matrix products, bdot(): return jnp.dot(first_op, second_op, preferred_element_type=jnp.float32)  67.8 us
    psum x1, blocking collectives, per_device(): lax.psum((grad_col_bias, grad_out_bias, grad_gain_one, grad_shift_one, gr...  45.1 us
    reduce_scatter x1, waiting for transfers between devices, per_device(): lax.psum_scatter(hidden_terms, 'mp', scatter_dimension=0, tiled=True)  44.6 us
    reduce_scatter x1, waiting for transfers between devices, per_device(): lax.psum_scatter(bdot(active, w_down), 'mp', scatter_dimension=0, tiled=T...  41.3 us
    all_gather x1, waiting for transfers between devices, per_device(): lax.all_gather(col_vec, ('tower', 'mp'), axis=0, tiled=True)  36.2 us
    ppermute x2, waiting for transfers between devices, from_partner(): return lax.ppermute(block, axis, route)  29.2 us
  transfers between devices with their start and end apart: 14, of which 12 were waited for; matrix products, arithmetic and copies ran while one was open for 8% of the time, Pallas kernels for 0%

commit v1 on v0

v1 whole, which is shorter than its diff:
```python
import math

import jax
import jax.numpy as jnp
from jax import lax
from jax.sharding import PartitionSpec as P

HEAD_DIM = 64
EPS = 1e-05
NORM_EPS = 1e-06
SCALE_DENSE = 50.0
SCALE_COL = 50.0
SHARP = 20.0
BLOCK_ROWS = 512
HIGH = lax.Precision.HIGHEST
BF = jnp.bfloat16
F32 = jnp.float32


def swap(block, axis, bit):
    count = lax.axis_size(axis)
    return lax.ppermute(block, axis, [(low, low ^ bit) for low in range(count)])


def gather_mp(own):
    near = swap(own, "mp", 1)
    far = swap(own, "mp", 2)
    return own, near, far, swap(far, "mp", 1)


def scatter_mp(own_half, far_half):
    count = own_half.shape[0] // 2
    far_sum = far_half[:count] + swap(far_half[count:].astype(BF), "mp", 1).astype(F32)
    arrived = swap(far_sum.astype(BF), "mp", 2)
    own_sum = own_half[:count] + swap(own_half[count:].astype(BF), "mp", 1).astype(F32)
    return own_sum + arrived.astype(F32)


def dp_bits():
    return [1 << k for k in range(int(math.log2(lax.axis_size("dp"))))]


def sum_rest(value, dim):
    hops = [("tower", 1)] + [("dp", bit) for bit in dp_bits()]
    value = value.astype(BF)
    for axis, bit in hops:
        half = value.shape[dim] // 2
        side = jnp.minimum(lax.axis_index(axis) & bit, 1)
        send = lax.dynamic_slice_in_dim(value, (1 - side) * half, half, dim)
        keep = lax.dynamic_slice_in_dim(value, side * half, half, dim)
        value = (keep.astype(F32) + swap(send, axis, bit).astype(F32)).astype(BF)
    for axis, bit in hops[::-1]:
        other = swap(value, axis, bit)
        first = (lax.axis_index(axis) & bit) == 0
        value = jnp.where(
            first,
            lax.concatenate([value, other], dim),
            lax.concatenate([other, value], dim),
        )
    return value.astype(F32)


def sum_small(value, hops):
    for axis, bit in hops:
        value = value + swap(value, axis, bit)
    return value


def relative(values, mp_index):
    shape = values.shape
    blocks = values.reshape(shape[:-1] + (2, 2, shape[-1] // 4))
    blocks = jnp.where(mp_index & 1, blocks[..., ::-1, :], blocks)
    blocks = jnp.where(mp_index & 2, blocks[..., ::-1, :, :], blocks)
    return blocks.reshape(shape)


def bdot(first_op, second_op):
    return jnp.dot(first_op, second_op, preferred_element_type=F32)


def nt_dot(first_op, second_op, precision=None):
    return lax.dot_general(
        first_op, second_op, (((1,), (1,)), ((), ())), precision=precision, preferred_element_type=F32
    )


def tn_dot(first_op, second_op, precision=None):
    return lax.dot_general(
        first_op, second_op, (((0,), (0,)), ((), ())), precision=precision, preferred_element_type=F32
    )


def fdot(first_op, second_op):
    return jnp.dot(first_op, second_op, precision=HIGH)


def norm_rows(values):
    row_mean = jnp.mean(values, axis=-1, keepdims=True)
    centred = values - row_mean
    scale = lax.rsqrt(jnp.mean(centred * centred, axis=-1, keepdims=True) + EPS)
    return centred * scale, scale


def norm_back(grad, normed, scale, gain_vec):
    scaled = grad * gain_vec
    mean_one = jnp.mean(scaled, axis=-1, keepdims=True)
    mean_two = jnp.mean(scaled * normed, axis=-1, keepdims=True)
    back = scale * (scaled - mean_one - normed * mean_two)
    return back, jnp.sum(grad * normed, axis=0), jnp.sum(grad, axis=0)


def unit_rows(values):
    scale = lax.rsqrt(jnp.sum(values * values, axis=-1, keepdims=True) + NORM_EPS)
    return values * scale, scale


def unit_back(grad, unit, scale):
    return scale * (grad - unit * jnp.sum(grad * unit, axis=-1, keepdims=True))


def cross_entropy(logits, targets):
    columns = jnp.arange(logits.shape[1], dtype=jnp.int32)
    onehot = (targets[:, None] == columns[None, :]).astype(F32)
    row_top = jnp.max(logits, axis=1, keepdims=True)
    exp_terms = jnp.exp(logits - row_top)
    row_total = jnp.sum(exp_terms, axis=1, keepdims=True)
    losses = row_top[:, 0] + jnp.log(row_total[:, 0]) - jnp.sum(logits * onehot, axis=1)
    return (losses, exp_terms / row_total - onehot)


def attend_forward(query_rows, key_rows, value_rows, seg_row, is_valid):
    length = query_rows.shape[0]
    head_count = query_rows.shape[1] // HEAD_DIM
    block_rows = min(BLOCK_ROWS, length)
    blocks = length // block_rows
    key_heads = key_rows.reshape(length, head_count, HEAD_DIM)
    value_heads = value_rows.reshape(length, head_count, HEAD_DIM)

    def one_block(inputs):
        query_block, seg_block = inputs
        raw_scores = (
            jnp.einsum("qhd,khd->hqk", query_block, key_heads, preferred_element_type=F32) * 0.125
        )
        allowed = jnp.logical_and(seg_block[:, None] == seg_row[None, :], is_valid[None, :])
        masked = jnp.where(allowed[None], raw_scores, -1e30)
        row_top = jnp.max(masked, axis=-1, keepdims=True)
        exp_terms = jnp.exp(masked - row_top)
        row_total = jnp.sum(exp_terms, axis=-1, keepdims=True)
        attn_probs = (exp_terms / row_total).astype(BF)
        mixed_out = jnp.einsum("hqk,khd->qhd", attn_probs, value_heads, preferred_element_type=F32)
        return (mixed_out.astype(BF), (row_top + jnp.log(row_total))[..., 0])

    mixed_all, log_total = lax.map(
        one_block,
        (
            query_rows.reshape(blocks, block_rows, head_count, HEAD_DIM),
            seg_row.reshape(blocks, block_rows),
        ),
    )
    return (mixed_all.reshape(length, head_count * HEAD_DIM), log_total)


def attend_backward(query_rows, key_rows, value_rows, grad_mixed, seg_row, is_valid, log_total):
    length = query_rows.shape[0]
    head_count = query_rows.shape[1] // HEAD_DIM
    block_rows = min(BLOCK_ROWS, length)
    blocks = length // block_rows
    key_heads = key_rows.reshape(length, head_count, HEAD_DIM)
    value_heads = value_rows.reshape(length, head_count, HEAD_DIM)

    def one_block(carry, inputs):
        key_acc, value_acc = carry
        query_block, seg_block, grad_block, total_block = inputs
        raw_scores = (
            jnp.einsum("qhd,khd->hqk", query_block, key_heads, preferred_element_type=F32) * 0.125
        )
        allowed = jnp.logical_and(seg_block[:, None] == seg_row[None, :], is_valid[None, :])
        masked = jnp.where(allowed[None], raw_scores, -1e30)
        attn_probs = jnp.exp(masked - total_block[..., None])
        grad_probs = jnp.einsum("qhd,khd->hqk", grad_block, value_heads, preferred_element_type=F32)
        row_dot = jnp.sum(attn_probs * grad_probs, axis=-1, keepdims=True)
        grad_scores = (attn_probs * (grad_probs - row_dot)).astype(BF)
        grad_query = (
            jnp.einsum("hqk,khd->qhd", grad_scores, key_heads, preferred_element_type=F32) * 0.125
        )
        key_acc = (
            key_acc
            + jnp.einsum("hqk,qhd->khd", grad_scores, query_block, preferred_element_type=F32) * 0.125
        )
        value_acc = value_acc + jnp.einsum(
            "hqk,qhd->khd", attn_probs.astype(BF), grad_block, preferred_element_type=F32
        )
        return ((key_acc, value_acc), grad_query.astype(BF))

    zero_acc = jnp.zeros((length, head_count, HEAD_DIM), F32)
    shaped = (blocks, block_rows, head_count, HEAD_DIM)
    (key_acc, value_acc), grad_query = lax.scan(
        one_block,
        (zero_acc, zero_acc),
        (
            query_rows.reshape(shaped),
            seg_row.reshape(blocks, block_rows),
            grad_mixed.reshape(shaped),
            log_total,
        ),
    )
    flat_shape = (length, head_count * HEAD_DIM)
    return (
        grad_query.reshape(flat_shape),
        key_acc.reshape(flat_shape).astype(BF),
        value_acc.reshape(flat_shape).astype(BF),
    )


def gelu_pair(inner):
    cdf = 0.5 + 0.5 * lax.erf(inner * math.sqrt(0.5))
    density = jnp.exp(-0.5 * inner * inner) * (1.0 / math.sqrt(2.0 * math.pi))
    return (inner * cdf).astype(BF), (cdf + inner * density).astype(BF)


def per_device(
    tokens,
    segment_ids,
    key_mask,
    positives,
    w_qkv,
    b_qv,
    w_out,
    b_out,
    gain_one,
    shift_one,
    w_up,
    b_up,
    w_down,
    b_down,
    gain_two,
    shift_two,
    w_col,
    b_col,
):
    own_rows = tokens[0, 0]
    own_count, model_dim = own_rows.shape
    pair_count = 2 * own_count
    mp_index = lax.axis_index("mp")
    is_query = lax.axis_index("tower") == 0
    dp_index = lax.axis_index("dp")
    dp_size = lax.axis_size("dp")
    seg_count = positives.shape[1]
    labels = jnp.arange(seg_count, dtype=jnp.int32)
    rel = lambda values: relative(values, mp_index)

    seg_pair = segment_ids[:, 0]
    starts = jnp.concatenate(
        [jnp.ones((2, 1), bool), seg_pair[:, 1:] != seg_pair[:, :-1]], axis=1
    )
    valid_pair = jnp.logical_or(key_mask[:, 0] > 0, starts)
    seg_rel = rel(seg_pair)
    start_rel = rel(starts.astype(jnp.int32)) > 0
    valid_rel = rel(valid_pair.astype(jnp.int32)) > 0
    seg_row = jnp.where(is_query, seg_rel[0], seg_rel[1])
    is_valid = jnp.where(is_query, valid_rel[0], valid_rel[1])
    start_row = jnp.where(is_query, start_rel[0], start_rel[1])
    members = seg_rel[:, None, :] == labels[None, :, None]
    weights = jnp.logical_and(members, valid_rel[:, None, :]).astype(F32)
    weight_q, weight_p = weights[0], weights[1]
    size_q = jnp.sum(weight_q, axis=1, keepdims=True)
    own_pick = jnp.logical_and(
        seg_row[None, :own_count] == labels[:, None], start_row[None, :own_count]
    ).astype(F32)

    x_chunks = gather_mp(own_rows)
    w_three = jnp.transpose(w_qkv, (1, 0, 2))
    x_near = jnp.concatenate(x_chunks[:2])
    x_far = jnp.concatenate(x_chunks[2:])

    def project(rows):
        return (
            (bdot(rows, w_three[0]) + b_qv[0]).astype(BF),
            bdot(rows, w_three[1]).astype(BF),
            (bdot(rows, w_three[2]) + b_qv[1]).astype(BF),
        )

    near_qkv, far_qkv = project(x_near), project(x_far)
    query_rows, key_rows, value_rows = (
        jnp.concatenate([near, far]) for near, far in zip(near_qkv, far_qkv)
    )
    context, log_total = attend_forward(query_rows, key_rows, value_rows, seg_row, is_valid)
    attn_sum = scatter_mp(bdot(context[:pair_count], w_out), bdot(context[pair_count:], w_out))
    normed_one, scale_one = norm_rows(own_rows.astype(F32) + attn_sum + b_out)
    hidden = normed_one * gain_one + shift_one

    col_chunks = gather_mp(w_col)
    col_near = jnp.where(
        mp_index & 1,
        jnp.concatenate([col_chunks[1], col_chunks[0]]),
        jnp.concatenate([col_chunks[0], col_chunks[1]]),
    )
    col_far = jnp.where(
        mp_index & 1,
        jnp.concatenate([col_chunks[3], col_chunks[2]]),
        jnp.concatenate([col_chunks[2], col_chunks[3]]),
    )
    col_weight = jnp.where(
        mp_index & 2, jnp.concatenate([col_far, col_near]), jnp.concatenate([col_near, col_far])
    )

    h_chunks = gather_mp(hidden.astype(BF))
    h_near, h_far = jnp.concatenate(h_chunks[:2]), jnp.concatenate(h_chunks[2:])
    act_near, slope_near = gelu_pair(bdot(h_near, w_up) + b_up)
    act_far, slope_far = gelu_pair(bdot(h_far, w_up) + b_up)
    ffn_sum = scatter_mp(bdot(act_near, w_down), bdot(act_far, w_down))
    normed_two, scale_two = norm_rows(hidden + ffn_sum + b_down)
    final_rows = normed_two * gain_two + shift_two
    encoded = final_rows.astype(BF)

    col_unit, col_scale = unit_rows(bdot(encoded, col_weight) + b_col)
    col_vec = col_unit.astype(BF)
    cls_unit, cls_scale = unit_rows(fdot(own_pick, final_rows))
    cls_own = cls_unit.astype(BF)
    half = own_count // 2
    other_a = swap(col_vec[:half], "tower", 1)
    other_b = swap(col_vec[half:], "tower", 1)
    cls_pair = jnp.concatenate([cls_own, swap(cls_own, "tower", 1)])
    far_a = swap(other_a, "mp", 2)
    far_b = swap(other_b, "mp", 2)
    cls_pair = sum_small(cls_pair, [("mp", 2), ("mp", 1)])
    other_near = jnp.concatenate([other_a, other_b])
    other_far = jnp.concatenate([far_a, far_b])
    others = jnp.concatenate(
        [other_near, swap(other_near, "mp", 1), other_far, swap(other_far, "mp", 1)]
    )

    exp_terms = jnp.exp(SHARP * nt_dot(col_vec, others))
    zero_sums = jnp.zeros((seg_count, 3 * own_count), F32)
    sums_q = nt_dot(weight_p, exp_terms, HIGH)
    sums_p = jnp.dot(weight_p[:, :own_count], exp_terms, precision=HIGH)
    sum_terms = jnp.where(is_query, jnp.concatenate([sums_q, zero_sums], axis=1), sums_p)

    def flip(values, bit):
        blocks = values.reshape(seg_count, 2, 2, own_count)
        blocks = blocks[:, ::-1] if bit == 2 else blocks[:, :, ::-1]
        return blocks.reshape(values.shape)

    sum_terms = sum_terms + flip(swap(sum_terms, "mp", 2), 2)
    sum_terms = sum_terms + flip(swap(sum_terms, "mp", 1), 1)
    nearest = jnp.log(sum_terms) / SHARP
    pair_score = nt_dot(weight_q, nearest, HIGH) / size_q
    positive_row = lax.dynamic_index_in_dim(positives, dp_index, 0, keepdims=False)
    col_losses, col_grad = cross_entropy(pair_score * SCALE_COL, positive_row)
    grad_pair = col_grad / seg_count * SCALE_COL
    grad_nearest = tn_dot(grad_pair / size_q, weight_q, HIGH)
    grad_sums = grad_nearest / (SHARP * sum_terms)
    left = jnp.where(is_query, grad_sums[:, :own_count], weight_p[:, :own_count])
    right = jnp.where(is_query, weight_p, grad_sums)
    grad_similar = (tn_dot(left, right, HIGH) * exp_terms * SHARP).astype(BF)
    grad_vec = bdot(grad_similar, others)
    grad_col_pre = unit_back(grad_vec, col_unit, col_scale).astype(BF)

    cls_all = cls_pair[None]
    order = dp_index[None]
    for bit in dp_bits():
        cls_all = jnp.concatenate([cls_all, swap(cls_all, "dp", bit)])
        order = jnp.concatenate([order, order ^ bit])
    cls_all = cls_all.reshape(dp_size, 2, seg_count, model_dim)
    cls_mine = cls_all[:, 0].reshape(dp_size * seg_count, model_dim)
    cls_theirs = cls_all[:, 1].reshape(dp_size * seg_count, model_dim)
    queries = jnp.where(is_query, cls_mine, cls_theirs)
    passages = jnp.where(is_query, cls_theirs, cls_mine)
    dense_logits = nt_dot(queries, passages) * SCALE_DENSE
    blocks = jnp.arange(dp_size, dtype=jnp.int32)[:, None]
    targets = (blocks * seg_count + positives[order]).reshape(dp_size * seg_count)
    dense_losses, dense_grad = cross_entropy(dense_logits, targets)
    dense_grad = (dense_grad / seg_count).astype(BF)
    grad_q = bdot(dense_grad[:seg_count], passages)
    grad_p = tn_dot(dense_grad[:, :seg_count], queries)
    grad_cls = jnp.where(is_query, grad_q, grad_p) * SCALE_DENSE
    grad_final = tn_dot(own_pick, unit_back(grad_cls, cls_unit, cls_scale), HIGH)
    loss_share = (jnp.sum(dense_losses[:seg_count]) + jnp.sum(col_losses)) / seg_count

    grad_final = grad_final + nt_dot(grad_col_pre, col_weight)
    grad_two, grad_gain_two, grad_shift_two = norm_back(
        grad_final, normed_two, scale_two, gain_two
    )
    grad_down_bias = jnp.sum(grad_two, axis=0)
    grad_col_bias = jnp.sum(grad_col_pre.astype(F32), axis=0)

    g_chunks = gather_mp(grad_two.astype(BF))
    g_near, g_far = jnp.concatenate(g_chunks[:2]), jnp.concatenate(g_chunks[2:])
    inner_near = (nt_dot(g_near, w_down) * slope_near.astype(F32)).astype(BF)
    inner_far = (nt_dot(g_far, w_down) * slope_far.astype(F32)).astype(BF)
    hidden_share = scatter_mp(nt_dot(inner_near, w_up), nt_dot(inner_far, w_up))
    grad_one, grad_gain_one, grad_shift_one = norm_back(
        grad_two + hidden_share, normed_one, scale_one, gain_one
    )
    grad_out_bias = jnp.sum(grad_one, axis=0)

    grad_down = sum_rest(tn_dot(act_near, g_near) + tn_dot(act_far, g_far), 0)
    grad_up = sum_rest(tn_dot(h_near, inner_near) + tn_dot(h_far, inner_far), 0)
    grad_up_bias = jnp.sum(inner_near.astype(F32), axis=0) + jnp.sum(
        inner_far.astype(F32), axis=0
    )
    col_part = tn_dot(rel(encoded), grad_col_pre)
    grad_col = sum_rest(scatter_mp(col_part[:pair_count], col_part[pair_count:]), 0)

    a_chunks = gather_mp(grad_one.astype(BF))
    a_near, a_far = jnp.concatenate(a_chunks[:2]), jnp.concatenate(a_chunks[2:])
    grad_context = jnp.concatenate([nt_dot(a_near, w_out), nt_dot(a_far, w_out)]).astype(BF)
    grad_out = sum_rest(
        tn_dot(context[:pair_count], a_near) + tn_dot(context[pair_count:], a_far), 0
    )
    grads = attend_backward(
        query_rows, key_rows, value_rows, grad_context, seg_row, is_valid, log_total
    )
    grad_x = [
        sum(nt_dot(grad[part], w_three[c]) for c, grad in enumerate(grads))
        for part in (slice(0, pair_count), slice(pair_count, 2 * pair_count))
    ]
    grad_input = grad_one + scatter_mp(grad_x[0], grad_x[1])
    grad_qkv = jnp.stack(
        [tn_dot(x_near, grad[:pair_count]) + tn_dot(x_far, grad[pair_count:]) for grad in grads]
    )
    grad_qkv = jnp.transpose(sum_rest(grad_qkv, 1), (1, 0, 2))
    d_tokens = grad_input.astype(BF).reshape(1, 1, own_count, model_dim)

    rest_hops = [("tower", 1)] + [("dp", bit) for bit in dp_bits()]
    share = loss_share / (2 * lax.axis_size("mp"))
    shared = jnp.stack(
        [
            grad_col_bias,
            grad_out_bias,
            grad_gain_one,
            grad_shift_one,
            grad_down_bias,
            grad_gain_two,
            grad_shift_two,
            jnp.broadcast_to(share, (model_dim,)),
        ]
    )
    shared = sum_small(shared, [("mp", 2), ("mp", 1)])
    shared = sum_small(jnp.concatenate([shared, grad_up_bias[None]]), rest_hops)
    qv_bias = sum_small(
        jnp.stack([jnp.sum(grads[0].astype(F32), axis=0), jnp.sum(grads[2].astype(F32), axis=0)]),
        rest_hops,
    )
    return (
        encoded.reshape(1, 1, own_count, model_dim),
        shared[7, 0],
        pair_score.reshape(1, seg_count, seg_count),
        d_tokens,
        grad_qkv,
        qv_bias,
        grad_out,
        shared[1],
        shared[2],
        shared[3],
        grad_up,
        shared[8],
        grad_down,
        shared[4],
        shared[5],
        shared[6],
        grad_col,
        shared[0],
    )


def solution(mesh):
    return jax.shard_map(
        per_device,
        mesh=mesh,
        in_specs=(
            P("tower", "dp", "mp", None),
            P(None, "dp", None),
            P(None, "dp", None),
            P(),
            P(None, None, "mp"),
            P(None, "mp"),
            P("mp", None),
            P(),
            P(),
            P(),
            P(None, "mp"),
            P("mp"),
            P("mp", None),
            P(),
            P(),
            P(),
            P("mp", None),
            P(),
        ),
        out_specs=(
            P("tower", "dp", "mp", None),
            P(),
            P("dp", None, None),
            P("tower", "dp", "mp", None),
            P(None, None, "mp"),
            P(None, "mp"),
            P("mp", None),
            P(),
            P(),
            P(),
            P(None, "mp"),
            P("mp"),
            P("mp", None),
            P(),
            P(),
            P(),
            P("mp", None),
            P(),
        ),
        check_vma=False,
    )
```

time: 1070 us -> 533 us (0.50)
  waiting for transfers between devices: 732 us -> 225 us
  blocking collectives: 105 us -> 0 us
  starting transfers between devices: 3.05 us -> 67.3 us
  other arithmetic: 44 us -> 79.9 us
  matrix products: 115 us -> 94.9 us
  between operations: 18.7 us -> 4.79 us
    psum x2 -> x0, waiting for transfers between devices: 472 us -> none  [the longest x1 387 us: per_device(): lax.psum((grad_qkv, grad_qv_bias, grad_out, grad_up, grad_up_bias, grad_d...]
    ppermute x2 -> x81, waiting for transfers between devices: 29.2 us -> 225 us  [swap(): return lax.ppermute(block, axis, [(low, low ^ bit) for low in range(count)])]
    all_gather x5 -> x0, waiting for transfers between devices: 121 us -> none  [the longest x1 36.2 us: per_device(): lax.all_gather(col_vec, ('tower', 'mp'), axis=0, tiled=True)]
    reduce_scatter x5 -> x0, waiting for transfers between devices: 108 us -> none  [the longest x1 44.6 us: per_device(): lax.psum_scatter(hidden_terms, 'mp', scatter_dimension=0, tiled=True)]
    psum x3 -> x0, blocking collectives: 80.7 us -> none  [the longest x1 45.1 us: per_device(): lax.psum((grad_col_bias, grad_out_bias, grad_gain_one, grad_shift_one, gr...]
    ppermute x2 -> x81, starting transfers between devices: 2.09 us -> 67.3 us  [swap(): return lax.ppermute(block, axis, [(low, low ^ bit) for low in range(count)])]
    all_gather x2 -> x0, blocking collectives: 23.8 us -> none  [the longest x1 13.7 us: per_device(): lax.all_gather(cls_pair.reshape(tower_size * seg_count, model_dim), 'dp',...]
    convert_element_type x10 -> x35, other arithmetic: 10.5 us -> 29.5 us  [the longest x4 9.3 us: sum_rest(): return value.astype(F32)]
  transfers between devices with their start and end apart: 14 -> 81, of which waited for: 12 -> 38; matrix products, arithmetic and copies ran while one was open for 8% -> 31% of each run, Pallas kernels for 0% -> 0%
where the time goes in v1:
time: 533 us; the launch traced here: 524 us
  waiting for transfers between devices  225 us (42%)
  matrix products  94.9 us (18%)
  other arithmetic  79.9 us (15%)
  starting transfers between devices  67.3 us (13%)
  local copies, waits for them, and re-layouts  51.1 us (10%)
    ppermute x81, waiting for transfers between devices, swap(): return lax.ppermute(block, axis, [(low, low ^ bit) for low in range(count)])  225 us
    ppermute x81, starting transfers between devices, swap(): return lax.ppermute(block, axis, [(low, low ^ bit) for low in range(count)])  67.3 us
    dot_general x15, matrix products, bdot(): return jnp.dot(first_op, second_op, preferred_element_type=F32)  23.3 us
    dot_general x17, matrix products, tn_dot(): lax.dot_general(first_op, second_op, (((0,), (0,)), ((), ())), precision=...  22.4 us
    dot_general x17, matrix products, nt_dot(): lax.dot_general(first_op, second_op, (((1,), (1,)), ((), ())), precision=...  19 us
    unnamed x239, local copies, waits for them, and re-layouts  14.4 us
  transfers between devices with their start and end apart: 81, of which 38 were waited for; matrix products, arithmetic and copies ran while one was open for 31% of the time, Pallas kernels for 0%

profile of v1, /device:TPU:0, one launch (start us, length us, event | category | flops | bytes accessed | tf_op | source)
XLA Modules:
  0.0 523.8 jit_solution(3095559164958788306)
XLA Ops:
  7.2 9.2 %collective-permute-done.1 = bf16[256,1024]{1,0:T(8,128)(2,1)S(1)} collective-permute-done((bf16[256,1024]{1,0:T(8,128)(2,1)}, bf16[256,1024]{1,0:T(8,128)(2,1)S(1)}, u32[]{:S(2)}, u32[]{:S(2)}) %collective-permute-start.1) | collective-permute-done | bytes 524320 | tf_op jit(solution)/shard_map/ppermute | solution.py:22
  31.0 16.6 %while.27 = (s32[]{:T(128)}, bf16[2,512,4,64]{1,3,2,0:T(8,128)(2,1)}, f32[2,4,512]{2,1,0:T(4,128)S(1)}, s32[2,512]{1,0:T(2,128)S(1)}, s32[1024]{0:T(1024)S(1)}, ...) while((s32[]{:T(128)}, ...), condition=%wide.region_3.4_spmd, body=%wide.region_0.3_spmd.sunk | while | flops 563214336 | bytes 35204304 | solution.py:153
  58.0 12.6 %collective-permute-done.5 = bf16[256,1024]{1,0:T(8,128)(2,1)} collective-permute-done((bf16[256,1024]{1,0:T(8,128)(2,1)}, bf16[256,1024]{1,0:T(8,128)(2,1)}, u32[]{:S(2)}, u32[]{:S(2)}) %collective-permute-start.5) | collective-permute-done | bytes 524320 | tf_op jit(solution)/shard_map/ppermute | solution.py:22
  76.2 16.3 %collective-permute-done.8 = bf16[256,1024]{1,0:T(8,128)(2,1)S(1)} collective-permute-done((bf16[256,1024]{1,0:T(8,128)(2,1)S(1)}, bf16[256,1024]{1,0:T(8,128)(2,1)S(1)}, u32[]{:S(2)}, u32[]{:S(2)}) %collective-permute-start.8) | collective-permute-done | bytes 524320 | tf_op jit(solution)/shard_map/ppermute | solution.py:22
  95.9 4.7 multiply_convert_fusion.4
  121.2 6.5 %collective-permute-done.11 = bf16[256,1024]{1,0:T(8,128)(2,1)} collective-permute-done((bf16[256,1024]{1,0:T(8,128)(2,1)}, bf16[256,1024]{1,0:T(8,128)(2,1)}, u32[]{:S(2)}, u32[]{:S(2)}) %collective-permute-start.11) | collective-permute-done | bytes 524320 | tf_op jit(solution)/shard_map/ppermute | solution.py:22
  141.8 6.1 %rev.38 = bf16[256,2,2,256]{3,2,1,0:T(2,128)(2,1)} reverse(bf16[256,2,2,256]{3,2,1,0:T(2,128)(2,1)} %reshape.540), dimensions={2} | reverse | bytes 1048576 | tf_op jit(solution)/shard_map/rev | solution.py:72
  165.6 4.5 collective-permute-done.16
  174.6 3.9 collective-permute-done.19
  178.6 3.6 collective-permute-done.18
  220.9 7.6 %collective-permute-done.30 = bf16[256,1024]{1,0:T(8,128)(2,1)} collective-permute-done((bf16[256,1024]{1,0:T(8,128)(2,1)}, bf16[256,1024]{1,0:T(8,128)(2,1)}, u32[]{:S(2)}, u32[]{:S(2)}) %collective-permute-start.30) | collective-permute-done | bytes 524320 | tf_op jit(solution)/shard_map/ppermute | solution.py:22
  228.5 3.7 convert_reduce_fusion.1
  247.2 5.6 %collective-permute-done.75 = bf16[128,1024]{1,0:T(8,128)(2,1)S(1)} collective-permute-done((bf16[128,1024]{1,0:T(8,128)(2,1)S(1)}, bf16[128,1024]{1,0:T(8,128)(2,1)S(1)}, u32[]{:S(2)}, u32[]{:S(2)}) %collective-permute-start.75) | collective-permute-done | bytes 262176 | tf_op jit(solution)/shard_map/ppermute | solution.py:22
  260.0 3.2 collective-permute-done.77
  265.1 3.3 collective-permute-done.78
  279.3 18.4 %collective-permute-done.66 = bf16[512,1024]{1,0:T(8,128)(2,1)S(1)} collective-permute-done((bf16[512,1024]{1,0:T(8,128)(2,1)S(1)}, bf16[512,1024]{1,0:T(8,128)(2,1)S(1)}, u32[]{:S(2)}, u32[]{:S(2)}) %collective-permute-start.66) | collective-permute-done | bytes 1048608 | tf_op jit(solution)/shard_map/ppermute | solution.py:22
  303.6 10.0 %collective-permute-done.67 = bf16[256,1024]{1,0:T(8,128)(2,1)S(1)} collective-permute-done((bf16[256,1024]{1,0:T(8,128)(2,1)S(1)}, bf16[256,1024]{1,0:T(8,128)(2,1)S(1)}, u32[]{:S(2)}, u32[]{:S(2)}) %collective-permute-start.67) | collective-permute-done | bytes 524320 | tf_op jit(solution)/shard_map/ppermute | solution.py:22
  317.3 12.8 %collective-permute-done.62 = bf16[128,1024]{1,0:T(8,128)(2,1)S(1)} collective-permute-done((bf16[128,1024]{1,0:T(8,128)(2,1)S(1)}, bf16[128,1024]{1,0:T(8,128)(2,1)S(1)}, u32[]{:S(2)}, u32[]{:S(2)}) %collective-permute-start.62) | collective-permute-done | bytes 262176 | tf_op jit(solution)/shard_map/ppermute | solution.py:22
  330.3 11.1 %collective-permute-done.68 = bf16[128,1024]{1,0:T(8,128)(2,1)S(1)} collective-permute-done((bf16[128,1024]{1,0:T(8,128)(2,1)S(1)}, bf16[128,1024]{1,0:T(8,128)(2,1)S(1)}, u32[]{:S(2)}, u32[]{:S(2)}) %collective-permute-start.68) | collective-permute-done | bytes 262176 | tf_op jit(solution)/shard_map/ppermute | solution.py:22
  342.0 4.9 collective-permute-done.63
  347.9 4.4 collective-permute-done.69
  358.8 25.5 %while.28 = (s32[]{:T(128)}, f32[1024,4,64]{0,2,1:T(8,128)S(1)}, f32[1024,4,64]{0,2,1:T(8,128)}, bf16[2,512,4,64]{1,3,2,0:T(8,128)(2,1)}, bf16[2,512,4,64]{1,3,2...) while((s32[]{:T(128)}, f32[1024,4,64]{0,2,1:T(8,128)S(1)}, ...), condition=%wide.region_36.37_spmd.clone, body=%wide.region_34.36_spmd.clone.sunk | while | flops 1376253952 | bytes 86838592 | solution.py:197
  363.5 3.2 multiply_reduce_fusion.15
  376.0 3.2 multiply_reduce_fusion.15
  408.0 4.4 collective-permute-done.55
  412.5 7.4 %collective-permute-done.45 = bf16[3,512,256]{2,1,0:T(8,128)(2,1)S(1)} collective-permute-done((bf16[3,512,256]{2,1,0:T(8,128)(2,1)S(1)}, bf16[3,512,256]{2,1,0:T(8,128)(2,1)S(1)}, u32[]{:S(2)}, u32[]{:S(2)}) %collective-permute-start.45) | collective-permute-done | bytes 786464 | tf_op jit(solution)/shard_map/ppermute | solution.py:22
  429.5 3.6 collective-permute-done.46
  441.6 6.6 %collective-permute-done.70 = bf16[256,1024]{1,0:T(8,128)(2,1)} collective-permute-done((bf16[256,1024]{1,0:T(8,128)(2,1)}, bf16[256,1024]{1,0:T(8,128)(2,1)}, u32[]{:S(2)}, u32[]{:S(2)}) %collective-permute-start.70) | collective-permute-done | bytes 524320 | tf_op jit(solution)/shard_map/ppermute | solution.py:22
  457.8 8.1 %collective-permute-done.48 = bf16[3,128,256]{2,1,0:T(8,128)(2,1)S(1)} collective-permute-done((bf16[3,128,256]{2,1,0:T(8,128)(2,1)S(1)}, bf16[3,128,256]{2,1,0:T(8,128)(2,1)S(1)}, u32[]{:S(2)}, u32[]{:S(2)}) %collective-permute-start.48) | collective-permute-done | bytes 196640 | tf_op jit(solution)/shard_map/ppermute | solution.py:22
  467.5 9.4 %collective-permute-done.36 = f32[9,1024]{1,0:T(8,128)S(1)} collective-permute-done((f32[9,1024]{1,0:T(8,128)S(1)}, f32[9,1024]{1,0:T(8,128)S(1)}, u32[]{:S(2)}, u32[]{:S(2)}) %collective-permute-start.36) | collective-permute-done | bytes 36896 | tf_op jit(solution)/shard_map/ppermute | solution.py:22
  486.6 22.0 %collective-permute-done.59 = bf16[128,1024]{1,0:T(8,128)(2,1)S(1)} collective-permute-done((bf16[128,1024]{1,0:T(8,128)(2,1)S(1)}, bf16[128,1024]{1,0:T(8,128)(2,1)S(1)}, u32[]{:S(2)}, u32[]{:S(2)}) %collective-permute-start.59) | collective-permute-done | bytes 262176 | tf_op jit(solution)/shard_map/ppermute | solution.py:22
  516.6 4.8 collective-permute-done.50
  (674 shorter events, 292.9 us)
Async XLA Ops:
  0.7 15.8 %collective-permute-start = (bf16[256,1024]{1,0:T(8,128)(2,1)}, bf16[256,1024]{1,0:T(8,128)(2,1)S(1)}, u32[]{:S(2)}, u32[]{:S(2)}) collective-permute-start(bf16[256,1024]{1,0:T(8,128)(2,1)} %bitcast.304), channel_id=1, source_target_pairs={{0,1},{1,0},{2,3},{3,2},{4,5},{5,4},{6,7},{7,6},{8,9},{9,8},{10,11... | collective-permute-start | bytes 1572872 | tf_op jit(solution)/shard_map/ppermute | solution.py:22
  57.3 48.1 %collective-permute-start.12 = (bf16[256,1024]{1,0:T(8,128)(2,1)}, bf16[256,1024]{1,0:T(8,128)(2,1)}, u32[]{:S(2)}, u32[]{:S(2)}) collective-permute-start(bf16[256,1024]{1,0:T(8,128)(2,1)} %param.38), channel_id=1, source_target_pairs={{0,2},{1,3},{2,0},{3,1},{4,6},{5,7},{6,4},{7,5},{8,10},{9,11},{10,... | collective-permute-start | bytes 1572872 | tf_op jit(solution)/shard_map/ppermute | solution.py:22
  57.6 59.0 %collective-permute-start.14 = (bf16[256,1024]{1,0:T(8,128)(2,1)}, bf16[256,1024]{1,0:T(8,128)(2,1)}, u32[]{:S(2)}, u32[]{:S(2)}) collective-permute-start(bf16[256,1024]{1,0:T(8,128)(2,1)} %param.38), channel_id=1, source_target_pairs={{0,1},{1,0},{2,3},{3,2},{4,5},{5,4},{6,7},{7,6},{8,9},{9,8},{10,11... | collective-permute-start | bytes 1572872 | tf_op jit(solution)/shard_map/ppermute | solution.py:22
  73.6 19.0 %collective-permute-start.8 = (bf16[256,1024]{1,0:T(8,128)(2,1)S(1)}, bf16[256,1024]{1,0:T(8,128)(2,1)S(1)}, u32[]{:S(2)}, u32[]{:S(2)}) collective-permute-start(bf16[256,1024]{1,0:T(8,128)(2,1)S(1)} %fusion.88), channel_id=1, source_target_pairs={{0,2},{1,3},{2,0},{3,1},{4,6},{5,7},{6,4},{7,5},{8,10},{9,11},{10,... | collective-permute-start | bytes 1572872 | tf_op jit(solution)/shard_map/ppermute | solution.py:22
  215.2 26.7 %collective-permute-start.72 = (bf16[256,1024]{1,0:T(8,128)(2,1)}, bf16[256,1024]{1,0:T(8,128)(2,1)}, u32[]{:S(2)}, u32[]{:S(2)}) collective-permute-start(bf16[256,1024]{1,0:T(8,128)(2,1)} %get-tuple-element.287), channel_id=1, source_target_pairs={{0,1},{1,0},{2,3},{3,2},{4,5},{5,4},{6,7},{7,6},{8,9},{9,8},{10,11... | collective-permute-start | bytes 1572872 | tf_op jit(solution)/shard_map/ppermute | solution.py:22
  219.3 22.6 %collective-permute-start.74 = (bf16[256,1024]{1,0:T(8,128)(2,1)S(1)}, bf16[256,1024]{1,0:T(8,128)(2,1)S(1)}, u32[]{:S(2)}, u32[]{:S(2)}) collective-permute-start(bf16[256,1024]{1,0:T(8,128)(2,1)S(1)} %fusion.70), channel_id=1, source_target_pairs={{0,2},{1,3},{2,0},{3,1},{4,6},{5,7},{6,4},{7,5},{8,10},{9,11},{10,... | collective-permute-start | bytes 1572872 | tf_op jit(solution)/shard_map/ppermute | solution.py:22
  241.3 30.1 %collective-permute-start.32 = (bf16[256,1024]{1,0:T(8,128)(2,1)S(1)}, bf16[256,1024]{1,0:T(8,128)(2,1)S(1)}, u32[]{:S(2)}, u32[]{:S(2)}) collective-permute-start(bf16[256,1024]{1,0:T(8,128)(2,1)S(1)} %slice.539), channel_id=1, source_target_pairs={{0,1},{1,0},{2,3},{3,2},{4,5},{5,4},{6,7},{7,6},{8,9},{9,8},{10,11... | collective-permute-start | bytes 1572872 | tf_op jit(solution)/shard_map/ppermute | solution.py:22
  246.6 30.1 %collective-permute-start.60 = (bf16[512,1024]{1,0:T(8,128)(2,1)S(1)}, bf16[512,1024]{1,0:T(8,128)(2,1)S(1)}, u32[]{:S(2)}, u32[]{:S(2)}) collective-permute-start(bf16[512,1024]{1,0:T(8,128)(2,1)S(1)} %constant_dynamic-slice_fusion.10), channel_id=1, source_target_pairs={{0,16},{16,0},{1,17},{17,1},{2,18},{18,2},{3,19},{19,3},{4,20},{20... | collective-permute-start | bytes 3145736 | tf_op jit(solution)/shard_map/ppermute | solution.py:22
  258.4 39.3 %collective-permute-start.66 = (bf16[512,1024]{1,0:T(8,128)(2,1)S(1)}, bf16[512,1024]{1,0:T(8,128)(2,1)S(1)}, u32[]{:S(2)}, u32[]{:S(2)}) collective-permute-start(bf16[512,1024]{1,0:T(8,128)(2,1)S(1)} %constant_dynamic-slice_fusion.7), channel_id=1, source_target_pairs={{0,16},{16,0},{1,17},{17,1},{2,18},{18,2},{3,19},{19,3},{4,20},{20... | collective-permute-start | bytes 3145736 | tf_op jit(solution)/shard_map/ppermute | solution.py:22
  265.0 34.8 %collective-permute-start.29 = (bf16[256,1024]{1,0:T(8,128)(2,1)S(1)}, bf16[256,1024]{1,0:T(8,128)(2,1)S(1)}, u32[]{:S(2)}, u32[]{:S(2)}) collective-permute-start(bf16[256,1024]{1,0:T(8,128)(2,1)S(1)} %slice.540), channel_id=1, source_target_pairs={{0,1},{1,0},{2,3},{3,2},{4,5},{5,4},{6,7},{7,6},{8,9},{9,8},{10,11... | collective-permute-start | bytes 1572872 | tf_op jit(solution)/shard_map/ppermute | solution.py:22
  271.6 28.2 %collective-permute-start.33 = (bf16[256,1024]{1,0:T(8,128)(2,1)S(1)}, bf16[256,1024]{1,0:T(8,128)(2,1)S(1)}, u32[]{:S(2)}, u32[]{:S(2)}) collective-permute-start(bf16[256,1024]{1,0:T(8,128)(2,1)S(1)} %fusion.77), channel_id=1, source_target_pairs={{0,2},{1,3},{2,0},{3,1},{4,6},{5,7},{6,4},{7,5},{8,10},{9,11},{10,... | collective-permute-start | bytes 1572872 | tf_op jit(solution)/shard_map/ppermute | solution.py:22
  275.2 202.0 %collective-permute-start.80 = (bf16[128,1024]{1,0:T(8,128)(2,1)}, bf16[128,1024]{1,0:T(8,128)(2,1)}, u32[]{:S(2)}, u32[]{:S(2)}) collective-permute-start(bf16[128,1024]{1,0:T(8,128)(2,1)} %maximum_select_fusion.17), channel_id=1, source_target_pairs={{0,16},{16,0},{1,17},{17,1},{2,18},{18,2},{3,19},{19,3},{4,20},{20... | collective-permute-start | bytes 786440 | tf_op jit(solution)/shard_map/ppermute | solution.py:22
  277.2 25.7 %collective-permute-start.61 = (bf16[256,1024]{1,0:T(8,128)(2,1)S(1)}, bf16[256,1024]{1,0:T(8,128)(2,1)S(1)}, u32[]{:S(2)}, u32[]{:S(2)}) collective-permute-start(bf16[256,1024]{1,0:T(8,128)(2,1)S(1)} %constant_dynamic-slice_fusion.9), channel_id=1, source_target_pairs={{0,4},{4,0},{8,12},{12,8},{1,5},{5,1},{9,13},{13,9},{2,6},{6,2},{1... | collective-permute-start | bytes 1572872 | tf_op jit(solution)/shard_map/ppermute | solution.py:22
  298.2 15.5 %collective-permute-start.67 = (bf16[256,1024]{1,0:T(8,128)(2,1)S(1)}, bf16[256,1024]{1,0:T(8,128)(2,1)S(1)}, u32[]{:S(2)}, u32[]{:S(2)}) collective-permute-start(bf16[256,1024]{1,0:T(8,128)(2,1)S(1)} %constant_dynamic-slice_fusion.6), channel_id=1, source_target_pairs={{0,4},{4,0},{8,12},{12,8},{1,5},{5,1},{9,13},{13,9},{2,6},{6,2},{1... | collective-permute-start | bytes 1572872 | tf_op jit(solution)/shard_map/ppermute | solution.py:22
  303.2 26.9 %collective-permute-start.62 = (bf16[128,1024]{1,0:T(8,128)(2,1)S(1)}, bf16[128,1024]{1,0:T(8,128)(2,1)S(1)}, u32[]{:S(2)}, u32[]{:S(2)}) collective-permute-start(bf16[128,1024]{1,0:T(8,128)(2,1)S(1)} %constant_dynamic-slice_fusion.8), channel_id=1, source_target_pairs={{0,8},{4,12},{8,0},{12,4},{1,9},{5,13},{9,1},{13,5},{2,10},{6,14},... | collective-permute-start | bytes 786440 | tf_op jit(solution)/shard_map/ppermute | solution.py:22
  313.9 27.4 %collective-permute-start.68 = (bf16[128,1024]{1,0:T(8,128)(2,1)S(1)}, bf16[128,1024]{1,0:T(8,128)(2,1)S(1)}, u32[]{:S(2)}, u32[]{:S(2)}) collective-permute-start(bf16[128,1024]{1,0:T(8,128)(2,1)S(1)} %constant_dynamic-slice_fusion.5), channel_id=1, source_target_pairs={{0,8},{4,12},{8,0},{12,4},{1,9},{5,13},{9,1},{13,5},{2,10},{6,14},... | collective-permute-start | bytes 786440 | tf_op jit(solution)/shard_map/ppermute | solution.py:22
  315.9 37.4 %collective-permute-start.41 = (bf16[256,1024]{1,0:T(8,128)(2,1)S(1)}, bf16[256,1024]{1,0:T(8,128)(2,1)S(1)}, u32[]{:S(2)}, u32[]{:S(2)}) collective-permute-start(bf16[256,1024]{1,0:T(8,128)(2,1)S(1)} %collective-permute-done.40), channel_id=1, source_target_pairs={{0,1},{1,0},{2,3},{3,2},{4,5},{5,4},{6,7},{7,6},{8,9},{9,8},{10,11... | collective-permute-start | bytes 1572872 | tf_op jit(solution)/shard_map/ppermute | solution.py:22
  330.2 16.8 %collective-permute-start.63 = (bf16[128,1024]{1,0:T(8,128)(2,1)S(1)}, bf16[128,1024]{1,0:T(8,128)(2,1)S(1)}, u32[]{:S(2)}, u32[]{:S(2)}) collective-permute-start(bf16[128,1024]{1,0:T(8,128)(2,1)S(1)} %add_convert_fusion.10), channel_id=1, source_target_pairs={{0,8},{4,12},{8,0},{12,4},{1,9},{5,13},{9,1},{13,5},{2,10},{6,14},... | collective-permute-start | bytes 786440 | tf_op jit(solution)/shard_map/ppermute | solution.py:22
  347.9 79.6 %collective-permute-start.64 = (bf16[256,1024]{1,0:T(8,128)(2,1)}, bf16[256,1024]{1,0:T(8,128)(2,1)}, u32[]{:S(2)}, u32[]{:S(2)}) collective-permute-start(bf16[256,1024]{1,0:T(8,128)(2,1)} %maximum_select_fusion.10), channel_id=1, source_target_pairs={{0,4},{4,0},{8,12},{12,8},{1,5},{5,1},{9,13},{13,9},{2,6},{6,2},{1... | collective-permute-start | bytes 1572872 | tf_op jit(solution)/shard_map/ppermute | solution.py:22
  401.0 18.9 %collective-permute-start.45 = (bf16[3,512,256]{2,1,0:T(8,128)(2,1)S(1)}, bf16[3,512,256]{2,1,0:T(8,128)(2,1)S(1)}, u32[]{:S(2)}, u32[]{:S(2)}) collective-permute-start(bf16[3,512,256]{2,1,0:T(8,128)(2,1)S(1)} %constant_dynamic-slice_fusion.16), channel_id=1, source_target_pairs={{0,16},{16,0},{1,17},{17,1},{2,18},{18,2},{3,19},{19,3},{4,20},{20... | collective-permute-start | bytes 2359304 | tf_op jit(solution)/shard_map/ppermute | solution.py:22
  403.6 16.6 %collective-permute-start.43 = (bf16[256,1024]{1,0:T(8,128)(2,1)S(1)}, bf16[256,1024]{1,0:T(8,128)(2,1)S(1)}, u32[]{:S(2)}, u32[]{:S(2)}) collective-permute-start(bf16[256,1024]{1,0:T(8,128)(2,1)S(1)} %slice.537), channel_id=1, source_target_pairs={{0,1},{1,0},{2,3},{3,2},{4,5},{5,4},{6,7},{7,6},{8,9},{9,8},{10,11... | collective-permute-start | bytes 1572872 | tf_op jit(solution)/shard_map/ppermute | solution.py:22
  412.4 23.7 %collective-permute-start.42 = (bf16[256,1024]{1,0:T(8,128)(2,1)S(1)}, bf16[256,1024]{1,0:T(8,128)(2,1)S(1)}, u32[]{:S(2)}, u32[]{:S(2)}) collective-permute-start(bf16[256,1024]{1,0:T(8,128)(2,1)S(1)} %slice.538), channel_id=1, source_target_pairs={{0,1},{1,0},{2,3},{3,2},{4,5},{5,4},{6,7},{7,6},{8,9},{9,8},{10,11... | collective-permute-start | bytes 1572872 | tf_op jit(solution)/shard_map/ppermute | solution.py:22
  427.5 20.7 %collective-permute-start.70 = (bf16[256,1024]{1,0:T(8,128)(2,1)}, bf16[256,1024]{1,0:T(8,128)(2,1)}, u32[]{:S(2)}, u32[]{:S(2)}) collective-permute-start(bf16[256,1024]{1,0:T(8,128)(2,1)} %maximum_select_fusion.11), channel_id=1, source_target_pairs={{0,4},{4,0},{8,12},{12,8},{1,5},{5,1},{9,13},{13,9},{2,6},{6,2},{1... | collective-permute-start | bytes 1572872 | tf_op jit(solution)/shard_map/ppermute | solution.py:22
  433.0 46.0 %collective-permute-start.53 = (f32[2,256]{1,0:T(2,128)}, f32[2,256]{1,0:T(2,128)}, u32[]{:S(2)}, u32[]{:S(2)}) collective-permute-start(f32[2,256]{1,0:T(2,128)} %fusion.268), channel_id=1, source_target_pairs={{0,8},{4,12},{8,0},{12,4},{1,9},{5,13},{9,1},{13,5},{2,10},{6,14},... | collective-permute-start | bytes 6152 | tf_op jit(solution)/shard_map/ppermute | solution.py:22
  436.1 17.9 %collective-permute-start.57 = (bf16[32,1024]{1,0:T(8,128)(2,1)}, bf16[32,1024]{1,0:T(8,128)(2,1)}, u32[]{:S(2)}, u32[]{:S(2)}) collective-permute-start(bf16[32,1024]{1,0:T(8,128)(2,1)} %add_convert_fusion.16), channel_id=1, source_target_pairs={{0,8},{4,12},{8,0},{12,4},{1,9},{5,13},{9,1},{13,5},{2,10},{6,14},... | collective-permute-start | bytes 196616 | tf_op jit(solution)/shard_map/ppermute | solution.py:22
  437.0 15.9 %collective-permute-start.47 = (bf16[3,128,256]{2,1,0:T(8,128)(2,1)}, bf16[3,128,256]{2,1,0:T(8,128)(2,1)}, u32[]{:S(2)}, u32[]{:S(2)}) collective-permute-start(bf16[3,128,256]{2,1,0:T(8,128)(2,1)} %constant_dynamic-slice_fusion.14), channel_id=1, source_target_pairs={{0,8},{4,12},{8,0},{12,4},{1,9},{5,13},{9,1},{13,5},{2,10},{6,14},... | collective-permute-start | bytes 589832 | tf_op jit(solution)/shard_map/ppermute | solution.py:22
  452.1 58.7 %collective-permute-start.65 = (bf16[512,1024]{1,0:T(8,128)(2,1)S(1)}, bf16[512,1024]{1,0:T(8,128)(2,1)S(1)}, u32[]{:S(2)}, u32[]{:S(2)}) collective-permute-start(bf16[512,1024]{1,0:T(8,128)(2,1)S(1)} %maximum_select_fusion.6), channel_id=1, source_target_pairs={{0,16},{16,0},{1,17},{17,1},{2,18},{18,2},{3,19},{19,3},{4,20},{20... | collective-permute-start | bytes 3145736 | tf_op jit(solution)/shard_map/ppermute | solution.py:22
  467.3 18.1 %collective-permute-start.49 = (bf16[3,256,256]{2,1,0:T(8,128)(2,1)S(1)}, bf16[3,256,256]{2,1,0:T(8,128)(2,1)S(1)}, u32[]{:S(2)}, u32[]{:S(2)}) collective-permute-start(bf16[3,256,256]{2,1,0:T(8,128)(2,1)S(1)} %maximum_select_fusion.13), channel_id=1, source_target_pairs={{0,4},{4,0},{8,12},{12,8},{1,5},{5,1},{9,13},{13,9},{2,6},{6,2},{1... | collective-permute-start | bytes 1179656 | tf_op jit(solution)/shard_map/ppermute | solution.py:22
  476.9 36.8 %collective-permute-start.71 = (bf16[512,1024]{1,0:T(8,128)(2,1)S(1)}, bf16[512,1024]{1,0:T(8,128)(2,1)S(1)}, u32[]{:S(2)}, u32[]{:S(2)}) collective-permute-start(bf16[512,1024]{1,0:T(8,128)(2,1)S(1)} %maximum_select_fusion.7), channel_id=1, source_target_pairs={{0,16},{16,0},{1,17},{17,1},{2,18},{18,2},{3,19},{19,3},{4,20},{20... | collective-permute-start | bytes 3145736 | tf_op jit(solution)/shard_map/ppermute | solution.py:22
  477.2 31.4 %collective-permute-start.59 = (bf16[128,1024]{1,0:T(8,128)(2,1)S(1)}, bf16[128,1024]{1,0:T(8,128)(2,1)S(1)}, u32[]{:S(2)}, u32[]{:S(2)}) collective-permute-start(bf16[128,1024]{1,0:T(8,128)(2,1)S(1)} %maximum_select_fusion.16), channel_id=1, source_target_pairs={{0,16},{16,0},{1,17},{17,1},{2,18},{18,2},{3,19},{19,3},{4,20},{20... | collective-permute-start | bytes 786440 | tf_op jit(solution)/shard_map/ppermute | solution.py:22
  484.0 25.7 %collective-permute-start.38 = (f32[9,1024]{1,0:T(8,128)S(1)}, f32[9,1024]{1,0:T(8,128)S(1)}, u32[]{:S(2)}, u32[]{:S(2)}) collective-permute-start(f32[9,1024]{1,0:T(8,128)S(1)} %add.498), channel_id=1, source_target_pairs={{0,8},{4,12},{8,0},{12,4},{1,9},{5,13},{9,1},{13,5},{2,10},{6,14},... | collective-permute-start | bytes 110600 | tf_op jit(solution)/shard_map/ppermute | solution.py:22
  485.7 35.6 %collective-permute-start.50 = (bf16[3,512,256]{2,1,0:T(8,128)(2,1)S(1)}, bf16[3,512,256]{2,1,0:T(8,128)(2,1)S(1)}, u32[]{:S(2)}, u32[]{:S(2)}) collective-permute-start(bf16[3,512,256]{2,1,0:T(8,128)(2,1)S(1)} %maximum_select_fusion.8), channel_id=1, source_target_pairs={{0,16},{16,0},{1,17},{17,1},{2,18},{18,2},{3,19},{19,3},{4,20},{20... | collective-permute-start | bytes 2359304 | tf_op jit(solution)/shard_map/ppermute | solution.py:22
  (178 other events, 1327.4 us)
